TPU v7x, 512 devices: a whole 4x8x8 slice. The times are simulated.
512 devices in a mesh: group: 16 (over x_hi, y), blk: 32 (over z, x_lo, core).
Axes of the slice: x: 4 (x_hi: 2, x_lo: 2; x = x_hi * 2 + x_lo), y: 8, z: 8, core: 2. Of those that a mesh axis runs over, the one named last changes fastest.
Arguments:
- queries: bfloat16 [32768, 2560], P(('group', 'blk')), may hold values from -6 to 6
- keys: bfloat16 [32768, 2560], P(('group', 'blk')), may hold values from -6 to 6
- values: bfloat16 [32768, 2560], P(('group', 'blk')), may hold values from -6 to 6
- stale_keys: bfloat16 [32768, 2560], P(('group', 'blk')), may hold values from -6 to 6
- stale_values: bfloat16 [32768, 2560], P(('group', 'blk')), may hold values from -6 to 6
- patch_order: int32 [32768], P(('group', 'blk')), may hold values from 0 to 63, as said below
- stale_age: int32 [16], replicated, may hold values from 0 to 3
Outputs:
- attended: bfloat16 [32768, 2560], P(('group', 'blk'))
Inputs may be any that keep to these rules, and one draw needn't show every extreme that they name: `patch_order`: each device's block of 64 entries is a permutation of 0 .. 63.
All inputs are finite; a program needn't handle non-finite values.
Results may differ from a plain program's by a relative error of at most 0.0046.
Values may be sent and summed in bfloat16 or wider, within the bound.
A program may use at most 64 MiB of HBM per device.

v0:
```python
import jax
import jax.numpy as jnp
from jax import lax
from jax.sharding import PartitionSpec as P

HEAD_DIM = 128
POOL = 4
REACH = 3


age_penalty = 0.5
masked = -1e30


def shifted(x, axis, by):
    size = lax.axis_size(axis)
    return lax.ppermute(x, axis, [(i, (i + by) % size) for i in range(size)])


def body(queries, keys, values, stale_keys, stale_values, patch_order, stale_age):
    rows, width = queries.shape
    heads = width // HEAD_DIM
    pooled_rows = rows // POOL
    groups = lax.axis_size("group")
    mine = lax.axis_index("group")
    stale_pair = jnp.stack([stale_keys, stale_values], axis=0)
    picked = jnp.take(stale_pair, patch_order, axis=1).astype(jnp.float32)
    pooled = jnp.mean(picked.reshape(2, pooled_rows, POOL, width), axis=2).astype(jnp.bfloat16)
    gathered = lax.all_gather(pooled, "group", axis=1, tiled=True)
    fresh_pair = jnp.stack([keys, values], axis=0)
    tiles = {0: fresh_pair}
    for offset in [d for d in range(-REACH, REACH + 1) if d != 0]:
        tiles[offset] = shifted(fresh_pair, "blk", -offset)
    group_ids = jnp.arange(groups, dtype=jnp.int32)
    group_bias = jnp.where(
        group_ids == mine, jnp.float32(masked), -age_penalty * stale_age.astype(jnp.float32)
    )
    pool_bias = jnp.repeat(group_bias, pooled_rows)
    scale = 1.0 / jnp.sqrt(jnp.float32(HEAD_DIM))
    query_heads = queries.reshape(rows, heads, HEAD_DIM)
    pieces = [tiles[d] for d in range(-REACH, REACH + 1)] + [gathered]
    score_list = []
    for index, piece in enumerate(pieces):
        count = piece.shape[1]
        key_heads = piece[0].reshape(count, heads, HEAD_DIM)
        scores = (
            jnp.einsum("qhd,khd->hqk", query_heads, key_heads, preferred_element_type=jnp.float32)
            * scale
        )
        if index == len(pieces) - 1:
            scores = scores + pool_bias[None, None, :]
        score_list.append(scores)
    peak = score_list[0].max(axis=-1, keepdims=True)
    for scores in score_list[1:]:
        peak = jnp.maximum(peak, scores.max(axis=-1, keepdims=True))
    total = jnp.zeros((heads, rows), jnp.float32)
    summed = jnp.zeros((rows, heads, HEAD_DIM), jnp.float32)
    for scores, piece in zip(score_list, pieces):
        count = piece.shape[1]
        expo = jnp.exp(scores - peak)
        total = total + jnp.sum(expo, axis=-1)
        weights = expo.astype(jnp.bfloat16)
        value_heads = piece[1].reshape(count, heads, HEAD_DIM)
        summed = summed + jnp.einsum(
            "hqk,khd->qhd", weights, value_heads, preferred_element_type=jnp.float32
        )
    result = summed / jnp.transpose(total)[:, :, None]
    return result.reshape(rows, width).astype(jnp.bfloat16)


def solution(mesh):
    return jax.shard_map(
        body,
        mesh=mesh,
        in_specs=(
            P(("group", "blk"), None),
            P(("group", "blk"), None),
            P(("group", "blk"), None),
            P(("group", "blk"), None),
            P(("group", "blk"), None),
            P(("group", "blk")),
            P(),
        ),
        out_specs=P(("group", "blk"), None),
        check_vma=False,
    )
```

profile of v0, /device:TPU:24, one launch (start us, length us, event | category | flops | bytes accessed | tf_op | source)
XLA Modules:
  0.0 174.7 jit_solution(14781177474012326909)
XLA Ops:
  6.6 2.1 %pad_maximum_fusion = bf16[2,64,2560]{2,1,0:T(8,128)(2,1)} fusion(bf16[1,64,2560]{2,1,0:T(8,128)(2,1)} %bitcast.138, bf16[1,64,2560]{2,1,0:T(8,128)(2,1)} %bitcast.137), kind=kLoop, calls=%fused_computation.38 | loop fusion | flops 327680 | bytes 1310720 | tf_op jit(solution)/shard_map/stack | solution.py:30
  8.6 10.4 %collective-permute-start.5 = (bf16[2,64,2560]{2,1,0:T(8,128)(2,1)}, bf16[2,64,2560]{2,1,0:T(8,128)(2,1)S(1)}, u32[]{:S(2)}, u32[]{:S(2)}) collective-permute-start(bf16[2,64,2560]{2,1,0:T(8,128)(2,1)} %pad_maximum_fusion), channel_id=1, source_target_pairs={{0,29},{1,30},{2,31},{3,0},{4,1},{5,2},{6,3},{7,4},{8,5},{9,6},{10... | collective-permute-start | bytes 1966088 | tf_op jit(solution)/shard_map/ppermute | solution.py:17
  19.0 3.4 %collective-permute-start.4 = (bf16[2,64,2560]{2,1,0:T(8,128)(2,1)}, bf16[2,64,2560]{2,1,0:T(8,128)(2,1)}, u32[]{:S(2)}, u32[]{:S(2)}) collective-permute-start(bf16[2,64,2560]{2,1,0:T(8,128)(2,1)} %pad_maximum_fusion), channel_id=1, source_target_pairs={{0,30},{1,31},{2,0},{3,1},{4,2},{5,3},{6,4},{7,5},{8,6},{9,7},{10,... | collective-permute-start | bytes 1966088 | tf_op jit(solution)/shard_map/ppermute | solution.py:17
  22.4 3.4 %collective-permute-start.3 = (bf16[2,64,2560]{2,1,0:T(8,128)(2,1)}, bf16[2,64,2560]{2,1,0:T(8,128)(2,1)S(1)}, u32[]{:S(2)}, u32[]{:S(2)}) collective-permute-start(bf16[2,64,2560]{2,1,0:T(8,128)(2,1)} %pad_maximum_fusion), channel_id=1, source_target_pairs={{0,31},{1,0},{2,1},{3,2},{4,3},{5,4},{6,5},{7,6},{8,7},{9,8},{10,9... | collective-permute-start | bytes 1966088 | tf_op jit(solution)/shard_map/ppermute | solution.py:17
  25.8 1.9 %collective-permute-start.2 = (bf16[2,64,2560]{2,1,0:T(8,128)(2,1)}, bf16[2,64,2560]{2,1,0:T(8,128)(2,1)}, u32[]{:S(2)}, u32[]{:S(2)}) collective-permute-start(bf16[2,64,2560]{2,1,0:T(8,128)(2,1)} %pad_maximum_fusion), channel_id=1, source_target_pairs={{0,1},{1,2},{2,3},{3,4},{4,5},{5,6},{6,7},{7,8},{8,9},{9,10},{10,1... | collective-permute-start | bytes 1966088 | tf_op jit(solution)/shard_map/ppermute | solution.py:17
  27.7 4.6 %collective-permute-start = (bf16[2,64,2560]{2,1,0:T(8,128)(2,1)}, bf16[2,64,2560]{2,1,0:T(8,128)(2,1)}, u32[]{:S(2)}, u32[]{:S(2)}) collective-permute-start(bf16[2,64,2560]{2,1,0:T(8,128)(2,1)} %pad_maximum_fusion), channel_id=1, source_target_pairs={{0,3},{1,4},{2,5},{3,6},{4,7},{5,8},{6,9},{7,10},{8,11},{9,12},{10... | collective-permute-start | bytes 1966088 | tf_op jit(solution)/shard_map/ppermute | solution.py:17
  32.4 0.5 copy.110
  33.0 0.5 copy.109
  33.5 1.5 pad_maximum_fusion.1
  35.0 1.9 %gather_fusion = bf16[64,2,2560]{2,1,0:T(2,128)(2,1)S(1)} fusion(bf16[2,64,2560]{2,0,1:T(2,128)(2,1)S(1)} %pad_maximum_fusion.1, s32[1024]{0:T(1024)S(1)} %pad_clamp_fusion), kind=kCustom, calls=%fused_computation | custom fusion | bytes 1310976 | tf_op jit(solution)/shard_map/jit(_take)/gather | solution.py:27
  36.9 1.1 convert_reduce_fusion
  38.0 0.8 multiply_convert_fusion
  39.0 1.2 fusion.95
  40.2 0.8 copy-done.15
  41.0 2.1 %collective-permute-start.1 = (bf16[2,64,2560]{2,1,0:T(8,128)(2,1)}, bf16[2,64,2560]{2,1,0:T(8,128)(2,1)}, u32[]{:S(2)}, u32[]{:S(2)}) collective-permute-start(bf16[2,64,2560]{2,1,0:T(8,128)(2,1)} %pad_maximum_fusion), channel_id=1, source_target_pairs={{0,2},{1,3},{2,4},{3,5},{4,6},{5,7},{6,8},{7,9},{8,10},{9,11},{10,... | collective-permute-start | bytes 1966088 | tf_op jit(solution)/shard_map/ppermute | solution.py:17
  43.1 1.1 fusion.85
  44.5 10.7 %collective-permute-done.4 = bf16[2,64,2560]{2,1,0:T(8,128)(2,1)} collective-permute-done((bf16[2,64,2560]{2,1,0:T(8,128)(2,1)}, bf16[2,64,2560]{2,1,0:T(8,128)(2,1)}, u32[]{:S(2)}, u32[]{:S(2)}) %collective-permute-start.4) | collective-permute-done | bytes 655392 | tf_op jit(solution)/shard_map/ppermute | solution.py:17
  55.2 1.8 %fusion.86 = (bf16[1,64,2560]{2,1,0:T(8,128)(2,1)}, bf16[1,64,2560]{2,1,0:T(8,128)(2,1)S(1)}) fusion(bf16[2,64,2560]{2,1,0:T(8,128)(2,1)} %collective-permute-done.4), kind=kLoop, calls=%fused_computation.113 | loop fusion | bytes 1310720 | tf_op jit(solution)/shard_map/slice | solution.py:63
  57.5 1.9 %fusion.90 = (bf16[1,64,2560]{2,1,0:T(8,128)(2,1)}, bf16[1,64,2560]{2,1,0:T(8,128)(2,1)S(1)}) fusion(bf16[2,64,2560]{2,1,0:T(8,128)(2,1)} %collective-permute-done.2), kind=kLoop, calls=%fused_computation.117 | loop fusion | bytes 1310720 | tf_op jit(solution)/shard_map/slice | solution.py:63
  59.6 5.1 %collective-permute-done = bf16[2,64,2560]{2,1,0:T(8,128)(2,1)} collective-permute-done((bf16[2,64,2560]{2,1,0:T(8,128)(2,1)}, bf16[2,64,2560]{2,1,0:T(8,128)(2,1)}, u32[]{:S(2)}, u32[]{:S(2)}) %collective-permute-start) | collective-permute-done | bytes 655392 | tf_op jit(solution)/shard_map/ppermute | solution.py:17
  64.7 1.8 %fusion.88 = (bf16[1,64,2560]{2,1,0:T(8,128)(2,1)}, bf16[1,64,2560]{2,1,0:T(8,128)(2,1)S(1)}) fusion(bf16[2,64,2560]{2,1,0:T(8,128)(2,1)} %collective-permute-done), kind=kLoop, calls=%fused_computation.115 | loop fusion | bytes 1310720 | tf_op jit(solution)/shard_map/slice | solution.py:63
  66.8 11.9 %collective-permute-done.1 = bf16[2,64,2560]{2,1,0:T(8,128)(2,1)} collective-permute-done((bf16[2,64,2560]{2,1,0:T(8,128)(2,1)}, bf16[2,64,2560]{2,1,0:T(8,128)(2,1)}, u32[]{:S(2)}, u32[]{:S(2)}) %collective-permute-start.1) | collective-permute-done | bytes 655392 | tf_op jit(solution)/shard_map/ppermute | solution.py:17
  78.7 2.0 %fusion.89 = (bf16[1,64,2560]{2,1,0:T(8,128)(2,1)}, bf16[1,64,2560]{2,1,0:T(8,128)(2,1)}) fusion(bf16[2,64,2560]{2,1,0:T(8,128)(2,1)} %collective-permute-done.1), kind=kLoop, calls=%fused_computation.116 | loop fusion | bytes 1310720 | tf_op jit(solution)/shard_map/slice | solution.py:63
  80.7 1.2 reshape_squeeze.44
  81.9 1.9 %reshape_squeeze.51 = bf16[64,20,128]{2,1,0:T(8,128)(2,1)} reshape(bf16[1,64,2560]{2,1,0:T(8,128)(2,1)} %get-tuple-element.23) | data formatting | bytes 655360 | tf_op jit(solution)/shard_map/reshape;squeeze | solution.py:63
  83.8 1.9 %reshape_squeeze.50 = bf16[64,20,128]{2,1,0:T(8,128)(2,1)} reshape(bf16[1,64,2560]{2,1,0:T(8,128)(2,1)} %get-tuple-element.21) | data formatting | bytes 655360 | tf_op jit(solution)/shard_map/reshape;squeeze | solution.py:63
  85.7 1.9 %reshape_squeeze.42 = bf16[64,20,128]{2,1,0:T(8,128)(2,1)} reshape(bf16[1,64,2560]{2,1,0:T(8,128)(2,1)} %get-tuple-element.19) | data formatting | bytes 655360 | tf_op jit(solution)/shard_map/reshape;squeeze | solution.py:63
  87.7 1.0 reshape_squeeze.52
  88.6 1.2 reshape_squeeze.53
  89.8 1.0 reshape_squeeze.54
  90.8 1.1 fusion.92
  91.9 1.1 fusion.93
  93.1 1.1 fusion.94
  94.2 1.2 fusion.96
  95.4 1.2 fusion.97
  96.6 1.2 fusion.98
  97.7 40.7 %all-gather.2.cloned.1.call-done = bf16[2,256,2560]{2,0,1:T(2,128)(2,1)} async-done(((bf16[2,16,2560]{2,0,1:T(2,128)(2,1)}), bf16[2,256,2560]{2,0,1:T(2,128)(2,1)}) %all-gather.2.cloned.1.call-update) | async-done | bytes 2621456 | tf_op jit(solution)/shard_map/all_gather | solution.py:29
  138.5 7.8 %fusion.84 = (bf16[1,256,2560]{2,0,1:T(2,128)(2,1)S(1)}, bf16[1,256,2560]{2,0,1:T(2,128)(2,1)}) fusion(bf16[2,256,2560]{2,0,1:T(2,128)(2,1)} %all-gather.2.cloned.1.call-done), kind=kLoop, calls=%fused_computation.111 | loop fusion | bytes 5242880 | tf_op jit(solution)/shard_map/slice | solution.py:45
  146.2 6.1 %copy.141 = bf16[1,256,2560]{1,2,0:T(8,128)(2,1)} copy(bf16[1,256,2560]{2,0,1:T(2,128)(2,1)} %get-tuple-element.12) | data formatting | bytes 2621440
  152.4 3.8 %copy.140 = bf16[1,256,2560]{1,2,0:T(8,128)(2,1)} copy(bf16[1,256,2560]{2,0,1:T(2,128)(2,1)S(1)} %get-tuple-element.11) | data formatting | bytes 2621440
  156.2 1.7 fusion.91
  158.4 0.8 copy-done.7
  159.2 0.6 convolution_bitcast_fusion.4
  162.4 0.6 copy-done.14
  163.4 0.7 copy-done.4
  164.8 0.9 fusion.24
  166.1 0.7 copy-done.16
  167.1 0.8 copy.242
  (66 shorter events, 6.1 us)
Async XLA Ops:
  6.5 32.5 %copy-start = (bf16[64,2560]{1,0:T(8,128)(2,1)S(1)}, bf16[64,2560]{1,0:T(8,128)(2,1)}, u32[]{:S(2)}) copy-start(bf16[64,2560]{1,0:T(8,128)(2,1)} %param.7) | copy-start | bytes 983044
  6.5 25.8 %copy-start.19 = (s32[64]{0:T(128)S(1)}, s32[64]{0:T(128)}, u32[]{:S(2)}) copy-start(s32[64]{0:T(128)} %param.12) | copy-start | bytes 772
  6.5 25.9 %copy-start.17 = (bf16[64,2560]{1,0:T(8,128)(2,1)S(1)}, bf16[64,2560]{1,0:T(8,128)(2,1)}, u32[]{:S(2)}) copy-start(bf16[64,2560]{1,0:T(8,128)(2,1)} %param.11) | copy-start | bytes 983044
  6.5 26.4 %copy-start.18 = (bf16[64,2560]{1,0:T(8,128)(2,1)S(1)}, bf16[64,2560]{1,0:T(8,128)(2,1)}, u32[]{:S(2)}) copy-start(bf16[64,2560]{1,0:T(8,128)(2,1)} %param.10) | copy-start | bytes 983044
  6.5 131.9 %all-gather.2.cloned.1.call-start = ((), (), s32[]{:S(2)}) async-start(), calls=%async_computation | async-start | bytes 2785280 | tf_op jit(solution)/shard_map/all_gather | solution.py:29
  8.6 31.5 %collective-permute-start.5 = (bf16[2,64,2560]{2,1,0:T(8,128)(2,1)}, bf16[2,64,2560]{2,1,0:T(8,128)(2,1)S(1)}, u32[]{:S(2)}, u32[]{:S(2)}) collective-permute-start(bf16[2,64,2560]{2,1,0:T(8,128)(2,1)} %pad_maximum_fusion), channel_id=1, source_target_pairs={{0,29},{1,30},{2,31},{3,0},{4,1},{5,2},{6,3},{7,4},{8,5},{9,6},{10... | collective-permute-start | bytes 1966088 | tf_op jit(solution)/shard_map/ppermute | solution.py:17
  19.0 36.2 %collective-permute-start.4 = (bf16[2,64,2560]{2,1,0:T(8,128)(2,1)}, bf16[2,64,2560]{2,1,0:T(8,128)(2,1)}, u32[]{:S(2)}, u32[]{:S(2)}) collective-permute-start(bf16[2,64,2560]{2,1,0:T(8,128)(2,1)} %pad_maximum_fusion), channel_id=1, source_target_pairs={{0,30},{1,31},{2,0},{3,1},{4,2},{5,3},{6,4},{7,5},{8,6},{9,7},{10,... | collective-permute-start | bytes 1966088 | tf_op jit(solution)/shard_map/ppermute | solution.py:17
  22.4 34.8 %collective-permute-start.3 = (bf16[2,64,2560]{2,1,0:T(8,128)(2,1)}, bf16[2,64,2560]{2,1,0:T(8,128)(2,1)S(1)}, u32[]{:S(2)}, u32[]{:S(2)}) collective-permute-start(bf16[2,64,2560]{2,1,0:T(8,128)(2,1)} %pad_maximum_fusion), channel_id=1, source_target_pairs={{0,31},{1,0},{2,1},{3,2},{4,3},{5,4},{6,5},{7,6},{8,7},{9,8},{10,9... | collective-permute-start | bytes 1966088 | tf_op jit(solution)/shard_map/ppermute | solution.py:17
  25.8 31.7 %collective-permute-start.2 = (bf16[2,64,2560]{2,1,0:T(8,128)(2,1)}, bf16[2,64,2560]{2,1,0:T(8,128)(2,1)}, u32[]{:S(2)}, u32[]{:S(2)}) collective-permute-start(bf16[2,64,2560]{2,1,0:T(8,128)(2,1)} %pad_maximum_fusion), channel_id=1, source_target_pairs={{0,1},{1,2},{2,3},{3,4},{4,5},{5,6},{6,7},{7,8},{8,9},{9,10},{10,1... | collective-permute-start | bytes 1966088 | tf_op jit(solution)/shard_map/ppermute | solution.py:17
  27.7 37.0 %collective-permute-start = (bf16[2,64,2560]{2,1,0:T(8,128)(2,1)}, bf16[2,64,2560]{2,1,0:T(8,128)(2,1)}, u32[]{:S(2)}, u32[]{:S(2)}) collective-permute-start(bf16[2,64,2560]{2,1,0:T(8,128)(2,1)} %pad_maximum_fusion), channel_id=1, source_target_pairs={{0,3},{1,4},{2,5},{3,6},{4,7},{5,8},{6,9},{7,10},{8,11},{9,12},{10... | collective-permute-start | bytes 1966088 | tf_op jit(solution)/shard_map/ppermute | solution.py:17
  35.0 3.9 %copy-start.20 = (s32[16]{0:T(128)S(1)}, s32[16]{0:T(128)}, u32[]{:S(2)}) copy-start(s32[16]{0:T(128)} %param.13) | copy-start | bytes 196
  35.0 4.0 %copy-start.13 = (bf16[64,2560]{1,0:T(8,128)(2,1)S(1)}, bf16[64,2560]{1,0:T(8,128)(2,1)}, u32[]{:S(2)}) copy-start(bf16[64,2560]{1,0:T(8,128)(2,1)} %param.8) | copy-start | bytes 983044
  40.2 0.8 copy-start.15
  41.0 37.7 %collective-permute-start.1 = (bf16[2,64,2560]{2,1,0:T(8,128)(2,1)}, bf16[2,64,2560]{2,1,0:T(8,128)(2,1)}, u32[]{:S(2)}, u32[]{:S(2)}) collective-permute-start(bf16[2,64,2560]{2,1,0:T(8,128)(2,1)} %pad_maximum_fusion), channel_id=1, source_target_pairs={{0,2},{1,3},{2,4},{3,5},{4,6},{5,7},{6,8},{7,9},{8,10},{9,11},{10,... | collective-permute-start | bytes 1966088 | tf_op jit(solution)/shard_map/ppermute | solution.py:17
  157.9 1.3 copy-start.7
  159.2 1.1 copy-start.6
  159.2 1.6 copy-start.1
  159.2 1.6 copy-start.10
  159.9 1.3 copy-start.2
  159.9 1.3 copy-start.11
  160.8 1.2 copy-start.5
  160.8 1.3 copy-start.12
  162.1 1.0 copy-start.14
  163.0 1.1 copy-start.4
  163.0 1.2 copy-start.9
  163.4 1.2 copy-start.3
  163.4 1.4 copy-start.8
  165.7 1.0 copy-start.16
Sparse Core Ops, SparseCore 0:
  38.9 99.4 all-gather.1
where the time goes:
time: 176 us; the launch traced here: 175 us
  waiting for transfers between devices  68.5 us (39%)
  local copies, waits for them, and re-layouts  46.6 us (26%)
  starting transfers between devices  25.7 us (15%)
  between operations  13.8 us (8%)
  matrix products  12.7 us (7%)
  other arithmetic  7.35 us (4%)
    all_gather x1, waiting for transfers between devices, body(): gathered = lax.all_gather(pooled, 'group', axis=1, tiled=True)  40.7 us
    ppermute x6, waiting for transfers between devices, shifted(): return lax.ppermute(x, axis, [(i, (i + by) % size) for i in range(size)])  27.8 us
    ppermute x6, starting transfers between devices, shifted(): return lax.ppermute(x, axis, [(i, (i + by) % size) for i in range(size)])  25.7 us
    unnamed x44, local copies, waits for them, and re-layouts  15.1 us
    dot_general x8, matrix products, body(): jnp.einsum('qhd,khd->hqk', query_heads, key_heads, preferred_element_type...  9.85 us
    another operation x6, local copies, waits for them, and re-layouts, body(): value_heads = piece[1].reshape(count, heads, HEAD_DIM)  8.91 us
    slice x6, local copies, waits for them, and re-layouts, body(): value_heads = piece[1].reshape(count, heads, HEAD_DIM)  8.68 us
    slice x1, local copies, waits for them, and re-layouts, body(): key_heads = piece[0].reshape(count, heads, HEAD_DIM)  7.77 us
  transfers between devices with their start and end apart: 7, of which 4 were waited for; matrix products, arithmetic and copies ran while one was open for 20% of the time, Pallas kernels for 0%

commit v1 on v0

v1 whole, which is shorter than its diff:
```python
import functools

import jax
import jax.numpy as jnp
from jax import lax
from jax.experimental import pallas as pl
from jax.experimental.pallas import tpu as pltpu
from jax.sharding import PartitionSpec as P

MESH = pl.DeviceIdType.MESH
HEAD_DIM = 128
POOL = 4
LOG2E = 1.4426950408889634
AGE_PENALTY = 0.5
MASKED = -1e30
UNROLL = 5

OWN, OTHER, X, XF, ZD, ZF, ZFF = 0, 64, 128, 192, 256, 384, 448
POOLED = {
    ("own", 0, 0): 320,
    ("par", 0, 0): 336,
    ("own", 1, 1): 352,
    ("own", 1, -1): 368,
    ("par", 1, 1): 512,
    ("par", 1, -1): 528,
    ("own", 2, 1): 544,
    ("own", 2, -1): 560,
    ("par", 2, 1): 576,
    ("par", 2, -1): 592,
    ("own", 3, 1): 608,
    ("own", 3, -1): 624,
    ("par", 3, 1): 640,
    ("par", 3, -1): 656,
    ("own", 4, 1): 672,
    ("par", 4, 1): 688,
}
ROWS = 704


def copy_ids():
    ids = {}
    for kv in (0, 1):
        for name in ("other", "x", "zd", "xf", "zf", "zff"):
            ids[(name, kv)] = len(ids)
        ids[("par0", kv)] = len(ids)
        for col in ("own", "par"):
            for dist in (1, 2, 3):
                for way in (1, -1):
                    ids[(col, dist, way, kv)] = len(ids)
            ids[(col, 4, 1, kv)] = len(ids)
    return ids


IDS = copy_ids()


def kernel(
    q_hbm, k_hbm, v_hbm, sk_hbm, sv_hbm, order_ref, age_ref, out_ref,
    kbuf, vbuf, q, sk, sv, acc, top, part, ssem, rsem, lsem,
):
    g, b = lax.axis_index("group"), lax.axis_index("blk")
    xh, y = g // 8, g % 8
    z, xl, c = b // 4, (b // 2) % 2, b % 2

    def at(xh_, y_, z_, xl_, c_):
        return (xh_ * 8 + y_, z_ * 4 + xl_ * 2 + c_)

    other = at(xh, y, z, xl, 1 - c)
    xpeer = at(xh, y, z, 1 - xl, c)
    zup, zdown = at(xh, y, (z + 1) % 8, xl, c), at(xh, y, (z + 7) % 8, xl, c)
    zdirect = at(xh, y, (z + 7 + 2 * c) % 8, xl, 1 - c)
    zforward = at(xh, y, (z + 1 + 6 * xl) % 8, xl, c)
    ynext = {1: at(xh, (y + 1) % 8, z, xl, c), -1: at(xh, (y + 7) % 8, z, xl, c)}
    partner = at(1 - xh, y, z, xl, c)

    barrier = pltpu.get_barrier_semaphore()
    everyone = (other, xpeer, zup, zdown, zdirect, ynext[1], ynext[-1], partner)
    for device in everyone:
        pl.semaphore_signal(barrier, inc=1, device_id=device, device_id_type=MESH)

    bufs = (kbuf, vbuf)
    fresh = (k_hbm, v_hbm)
    loads = [
        pltpu.make_async_copy(src, dst, lsem.at[i])
        for i, (src, dst) in enumerate(
            (
                (sk_hbm, sk),
                (sv_hbm, sv),
                (q_hbm, q),
                (k_hbm, kbuf.at[pl.ds(OWN, 64)]),
                (v_hbm, vbuf.at[pl.ds(OWN, 64)]),
            )
        )
    ]
    for load in loads:
        load.start()

    def rows(kv, slot, count):
        return bufs[kv].at[pl.ds(slot, count)]

    def remote(key, src, dst, device):
        i = IDS[key]
        return pltpu.make_async_remote_copy(
            src_ref=src, dst_ref=dst, send_sem=ssem.at[i], recv_sem=rsem.at[i],
            device_id=device, device_id_type=MESH,
        )

    sent = []

    def send(key, src, dst, device):
        copy = remote(key, src, dst, device)
        copy.start()
        sent.append(copy)

    def arrived(key, dst):
        remote(key, dst, dst, other).wait_recv()

    t = lax.broadcasted_iota(jnp.int32, (64, 64), 0)
    picks = jnp.where(t == order_ref[...], 1.0, 0.0).astype(jnp.bfloat16)
    j = lax.broadcasted_iota(jnp.int32, (16, 64), 0)
    r = lax.broadcasted_iota(jnp.int32, (16, 64), 1)
    quarter = jnp.where(r // POOL == j, 1.0 / POOL, 0.0).astype(jnp.bfloat16)
    average = lax.dot_general(
        quarter, picks, (((1,), (1,)), ((), ())), preferred_element_type=jnp.float32
    ).astype(jnp.bfloat16)
    mine = POOLED[("own", 0, 0)]
    for kv, stale in enumerate((sk, sv)):
        loads[kv].wait()
        bufs[kv][pl.ds(mine, 16), :] = jnp.dot(
            average, stale[...], preferred_element_type=jnp.float32
        ).astype(jnp.bfloat16)

    pl.semaphore_wait(barrier, len(everyone))

    for kv in (0, 1):
        block = rows(kv, mine, 16)
        for way in (1, -1):
            send(("own", 1, way, kv), block, rows(kv, POOLED[("own", 1, way)], 16), ynext[way])
        send(("par0", kv), block, rows(kv, POOLED[("par", 0, 0)], 16), partner)
    for kv in (0, 1):
        send(("other", kv), fresh[kv], rows(kv, OTHER, 64), other)
        send(("x", kv), fresh[kv], rows(kv, X, 64), xpeer)
        send(("zd", kv), fresh[kv], rows(kv, ZD, 64), zdirect)

    def pass_on(col, dist, way, kv):
        slot = POOLED[(col, dist, way)]
        if dist:
            arrived((col, dist, way, kv), rows(kv, slot, 16))
        if dist < 3:
            send((col, dist + 1, way, kv), rows(kv, slot, 16), rows(kv, POOLED[(col, dist + 1, way)], 16), ynext[way])
        elif kv == (0 if way == 1 else 1):
            send((col, 4, 1, kv), rows(kv, slot, 16), rows(kv, POOLED[(col, 4, 1)], 16), ynext[way])

    def ring(col, dist):
        for kv in (0, 1):
            for way in (1, -1):
                pass_on(col, dist, way, kv)

    lane = lax.broadcasted_iota(jnp.int32, (1, 128), 1)

    def penalty(slot):
        col, dist, way = slot
        if slot == ("own", 0, 0):
            return jnp.float32(MASKED * LOG2E)
        half = xh if col == "own" else 1 - xh
        group = half * 8 + (y + 8 - way * dist) % 8
        return age_ref[group].astype(jnp.float32) * jnp.float32(-AGE_PENALTY * LOG2E)

    def bias_of(start, count):
        found = [(o - start, s) for s, o in POOLED.items() if start <= o < start + count]
        if not found:
            return None
        bias = jnp.zeros((1, count), jnp.float32)
        for offset, slot in found:
            here = (lane[:, :count] >= offset) & (lane[:, :count] < offset + 16)
            bias = jnp.where(here, penalty(slot), bias)
        return bias

    scale = LOG2E / (HEAD_DIM ** 0.5)
    heads = q.shape[1] // HEAD_DIM

    def attend(start, count, first=False, last=False):
        bias = bias_of(start, count)

        def head(h):
            cols = pl.ds(pl.multiple_of(h * HEAD_DIM, HEAD_DIM), HEAD_DIM)
            s = lax.dot_general(
                q[:, cols], kbuf[pl.ds(start, count), cols], (((1,), (1,)), ((), ())),
                preferred_element_type=jnp.float32,
            ) * scale
            if bias is not None:
                s = s + bias
            peak = jnp.max(s, axis=-1, keepdims=True)
            if first:
                old, new = None, jnp.broadcast_to(peak, (64, HEAD_DIM))
            else:
                old = top[:, cols]
                new = jnp.maximum(old, peak)
            p = jnp.exp2(s - new[:, :count])
            add = jnp.dot(
                p.astype(jnp.bfloat16), vbuf[pl.ds(start, count), cols],
                preferred_element_type=jnp.float32,
            )
            if count < HEAD_DIM:
                p = jnp.concatenate([p, jnp.zeros((64, HEAD_DIM - count), jnp.float32)], axis=1)
            if first:
                total, value = p, add
            else:
                keep = jnp.exp2(old - new)
                total = part[:, cols] * keep + p
                value = acc[:, cols] * keep + add
            if last:
                total = jnp.sum(total, axis=-1, keepdims=True)
                out_ref[:, cols] = (value / total).astype(jnp.bfloat16)
            else:
                top[:, cols] = new
                part[:, cols] = total
                acc[:, cols] = value

        @pl.loop(0, heads // UNROLL)
        def _(step):
            for u in range(UNROLL):
                head(step * UNROLL + u)

    for load in loads[2:]:
        load.wait()
    for kv in (0, 1):
        arrived(("other", kv), rows(kv, OTHER, 64))
    attend(OWN, 128, first=True)
    for kv in (0, 1):
        arrived(("par0", kv), rows(kv, POOLED[("par", 0, 0)], 16))
        block = rows(kv, POOLED[("par", 0, 0)], 16)
        for way in (1, -1):
            send(("par", 1, way, kv), block, rows(kv, POOLED[("par", 1, way)], 16), ynext[way])
    ring("own", 1)
    for kv in (0, 1):
        tile = rows(kv, X, 64)
        arrived(("x", kv), tile)
        send(("zf", kv), tile, rows(kv, ZF, 64), zforward)
        send(("xf", kv), tile, rows(kv, XF, 64), other)
    for kv in (0, 1):
        arrived(("zd", kv), rows(kv, ZD, 64))
    attend(ZD, 128)
    ring("par", 1)
    ring("own", 2)
    for kv in (0, 1):
        arrived(("xf", kv), rows(kv, XF, 64))
    attend(X, 128)
    ring("par", 2)
    for kv in (0, 1):
        tile = rows(kv, ZF, 64)
        arrived(("zf", kv), tile)
        send(("zff", kv), tile, rows(kv, ZFF, 64), other)
    for kv in (0, 1):
        arrived(("zff", kv), rows(kv, ZFF, 64))
    attend(ZF, 128)
    ring("own", 3)
    attend(POOLED[("par", 1, 1)], 128)
    ring("par", 3)
    for kv in (0, 1):
        for col in ("own", "par"):
            arrived((col, 4, 1, kv), rows(kv, POOLED[(col, 4, 1)], 16))
    attend(POOLED[("par", 3, 1)], 64, last=True)
    for copy in sent:
        copy.wait_send()


def body(queries, keys, values, stale_keys, stale_values, patch_order, stale_age):
    rows, width = queries.shape
    copies = len(IDS)
    wide = (rows, width)
    return pl.pallas_call(
        kernel,
        out_shape=jax.ShapeDtypeStruct(wide, jnp.bfloat16),
        in_specs=[pl.BlockSpec(memory_space=pl.ANY)] * 5
        + [pl.BlockSpec(memory_space=pltpu.VMEM), pl.BlockSpec(memory_space=pltpu.SMEM)],
        out_specs=pl.BlockSpec(memory_space=pltpu.VMEM),
        scratch_shapes=[
            pltpu.VMEM((ROWS, width), jnp.bfloat16),
            pltpu.VMEM((ROWS, width), jnp.bfloat16),
            pltpu.VMEM(wide, jnp.bfloat16),
            pltpu.VMEM(wide, jnp.bfloat16),
            pltpu.VMEM(wide, jnp.bfloat16),
            pltpu.VMEM(wide, jnp.float32),
            pltpu.VMEM(wide, jnp.float32),
            pltpu.VMEM(wide, jnp.float32),
            pltpu.SemaphoreType.DMA((copies,)),
            pltpu.SemaphoreType.DMA((copies,)),
            pltpu.SemaphoreType.DMA((5,)),
        ],
        name="tile_attention",
        compiler_params=pltpu.CompilerParams(
            collective_id=0, has_side_effects=True, vmem_limit_bytes=56 * 1024 * 1024
        ),
    )(queries, keys, values, stale_keys, stale_values, patch_order.reshape(1, rows), stale_age)


def solution(mesh):
    tokens = P(("group", "blk"), None)
    return jax.shard_map(
        body,
        mesh=mesh,
        in_specs=(tokens, tokens, tokens, tokens, tokens, P(("group", "blk")), P()),
        out_specs=tokens,
        check_vma=False,
    )
```

time: 176 us -> 68.6 us (0.39)
  the two profiles are of different devices: /device:TPU:24 before, /device:TPU:1 now
where the time goes in v1:
time: 68.6 us; the launch traced here: 68.4 us
  Pallas kernels  66.7 us (97%)
  local copies, waits for them, and re-layouts  1.72 us (3%)
    pallas_call x1, Pallas kernels, body(): pl.pallas_call(kernel, out_shape=jax.ShapeDtypeStruct(wide, jnp.bfloat16)...  66.7 us
    unnamed x1, local copies, waits for them, and re-layouts  1.72 us

profile of v1, /device:TPU:1, one launch (start us, length us, event | category | flops | bytes accessed | tf_op | source)
XLA Modules:
  0.0 68.4 jit_solution(16956537107475956193)
XLA Ops:
  0.0 66.7 %tile_attention.1 = bf16[64,2560]{1,0:T(8,128)(2,1)} custom-call(bf16[64,2560]{1,0:T(8,128)(2,1)} %q_hbm.1, bf16[64,2560]{1,0:T(8,128)(2,1)} %k_hbm.1, bf16[64,2560]{1,0:T(8,128)(2,1)} %v_hbm.1, bf16[64,2560]{1,0:T(8,128)(2,1)} %sk_hbm.1, bf16[64,2560]{1,0:T(8,128)(2,1)} %sv_hbm.1, s32[1,64]{1,0:T(1,128)} %bitcast.1, s32[16]{0:T(128)} %age_ref.1), custom_call_target="tpu_custom_call" | custom-call | tf_op jit(solution)/shard_map/tile_attention/pallas_call | solution.py:272
  66.7 1.7 %copy.9 = bf16[64,2560]{1,0:T(8,128)(2,1)} copy(bf16[64,2560]{1,0:T(8,128)(2,1)} %tile_attention.1) | data formatting | bytes 655360

commit v2 on v1

--- a/solution.py
+++ b/solution.py
@@ -13,7 +13,8 @@
 LOG2E = 1.4426950408889634
 AGE_PENALTY = 0.5
 MASKED = -1e30
-UNROLL = 5
+UNROLL = 20
+PARTS = 2
 
 OWN, OTHER, X, XF, ZD, ZF, ZFF = 0, 64, 128, 192, 256, 384, 448
 POOLED = {
@@ -21,17 +22,17 @@
     ("par", 0, 0): 336,
     ("own", 1, 1): 352,
     ("own", 1, -1): 368,
-    ("par", 1, 1): 512,
-    ("par", 1, -1): 528,
-    ("own", 2, 1): 544,
-    ("own", 2, -1): 560,
-    ("par", 2, 1): 576,
-    ("par", 2, -1): 592,
-    ("own", 3, 1): 608,
-    ("own", 3, -1): 624,
-    ("par", 3, 1): 640,
-    ("par", 3, -1): 656,
-    ("own", 4, 1): 672,
+    ("own", 2, 1): 512,
+    ("own", 2, -1): 528,
+    ("own", 3, 1): 544,
+    ("own", 3, -1): 560,
+    ("own", 4, 1): 576,
+    ("par", 1, 1): 592,
+    ("par", 1, -1): 608,
+    ("par", 2, 1): 624,
+    ("par", 2, -1): 640,
+    ("par", 3, 1): 656,
+    ("par", 3, -1): 672,
     ("par", 4, 1): 688,
 }
 ROWS = 704
@@ -41,7 +42,8 @@
     ids = {}
     for kv in (0, 1):
         for name in ("other", "x", "zd", "xf", "zf", "zff"):
-            ids[(name, kv)] = len(ids)
+            for part in range(PARTS):
+                ids[(name, kv, part)] = len(ids)
         ids[("par0", kv)] = len(ids)
         for col in ("own", "par"):
             for dist in (1, 2, 3):
@@ -56,7 +58,7 @@
 
 def kernel(
     q_hbm, k_hbm, v_hbm, sk_hbm, sv_hbm, order_ref, age_ref, out_ref,
-    kbuf, vbuf, q, sk, sv, acc, top, part, ssem, rsem, lsem,
+    kbuf, vbuf, q, sk, sv, acc, top, part, ssem, rsem, lsem, zsem,
 ):
     g, b = lax.axis_index("group"), lax.axis_index("blk")
     xh, y = g // 8, g % 8
@@ -74,9 +76,19 @@
     partner = at(1 - xh, y, z, xl, c)
 
     barrier = pltpu.get_barrier_semaphore()
-    everyone = (other, xpeer, zup, zdown, zdirect, ynext[1], ynext[-1], partner)
-    for device in everyone:
-        pl.semaphore_signal(barrier, inc=1, device_id=device, device_id_type=MESH)
+    plane = (other, xpeer, ynext[1], ynext[-1], partner)
+    across = (zup, zdown, zdirect)
+    odd = z % 2
+
+    def signal(semaphore, devices):
+        for device in devices:
+            pl.semaphore_signal(semaphore, inc=1, device_id=device, device_id_type=MESH)
+
+    signal(barrier, plane)
+
+    @pl.when(odd == 0)
+    def _():
+        signal(barrier, across)
 
     bufs = (kbuf, vbuf)
     fresh = (k_hbm, v_hbm)
@@ -130,29 +142,71 @@
             average, stale[...], preferred_element_type=jnp.float32
         ).astype(jnp.bfloat16)
 
-    pl.semaphore_wait(barrier, len(everyone))
+    pl.semaphore_wait(barrier, len(plane) + len(across) * odd)
+
+    @pl.when(odd == 1)
+    def _():
+        signal(zsem, across)
 
     for kv in (0, 1):
         block = rows(kv, mine, 16)
         for way in (1, -1):
             send(("own", 1, way, kv), block, rows(kv, POOLED[("own", 1, way)], 16), ynext[way])
         send(("par0", kv), block, rows(kv, POOLED[("par", 0, 0)], 16), partner)
-    for kv in (0, 1):
-        send(("other", kv), fresh[kv], rows(kv, OTHER, 64), other)
-        send(("x", kv), fresh[kv], rows(kv, X, 64), xpeer)
-        send(("zd", kv), fresh[kv], rows(kv, ZD, 64), zdirect)
+    span = q.shape[1] // PARTS
+
+    def piece(ref, part):
+        return ref.at[:, pl.ds(part * span, span)]
+
+    def tile(kv, slot, part):
+        return piece(rows(kv, slot, 64), part)
+
+    every = [(kv, part) for kv in (0, 1) for part in range(PARTS)]
+    for kv, n in every:
+        source = piece(fresh[kv], n)
+        send(("x", kv, n), source, tile(kv, X, n), xpeer)
+        send(("other", kv, n), source, tile(kv, OTHER, n), other)
+
+    def open_z():
+        @pl.when(odd == 0)
+        def _():
+            pl.semaphore_wait(zsem, len(across))
+
+        for kv, n in every:
+            remote(("zd", kv, n), piece(fresh[kv], n), tile(kv, ZD, n), zdirect).start()
+
+    pl.when(z != 0)(open_z)
+
+    def landed(name, slot):
+        for kv, n in every:
+            arrived((name, kv, n), tile(kv, slot, n))
+
+    def pass_x(kv, part):
+        here = tile(kv, X, part)
+        arrived(("x", kv, part), here)
+        send(("zf", kv, part), here, tile(kv, ZF, part), zforward)
+        send(("xf", kv, part), here, tile(kv, XF, part), other)
+
+    def pass_z(kv, part):
+        here = tile(kv, ZF, part)
+        arrived(("zf", kv, part), here)
+        send(("zff", kv, part), here, tile(kv, ZFF, part), other)
 
     def pass_on(col, dist, way, kv):
-        slot = POOLED[(col, dist, way)]
-        if dist:
-            arrived((col, dist, way, kv), rows(kv, slot, 16))
+        here = rows(kv, POOLED[(col, dist, way)], 16)
+        arrived((col, dist, way, kv), here)
         if dist < 3:
-            send((col, dist + 1, way, kv), rows(kv, slot, 16), rows(kv, POOLED[(col, dist + 1, way)], 16), ynext[way])
-        elif kv == (0 if way == 1 else 1):
-            send((col, 4, 1, kv), rows(kv, slot, 16), rows(kv, POOLED[(col, 4, 1)], 16), ynext[way])
-
-    def ring(col, dist):
-        for kv in (0, 1):
+            send((col, dist + 1, way, kv), here, rows(kv, POOLED[(col, dist + 1, way)], 16), ynext[way])
+        elif col == "own" and kv == (0 if way == 1 else 1):
+            send((col, 4, 1, kv), here, rows(kv, POOLED[(col, 4, 1)], 16), ynext[way])
+
+    def pass_far(kv):
+        here = rows(kv, POOLED[("own", 4, 1)], 16)
+        arrived(("own", 4, 1, kv), here)
+        send(("par", 4, 1, kv), here, rows(kv, POOLED[("par", 4, 1)], 16), partner)
+
+    def ring(col, dist, kvs=(0, 1)):
+        for kv in kvs:
             for way in (1, -1):
                 pass_on(col, dist, way, kv)
 
@@ -182,85 +236,93 @@
     def attend(start, count, first=False, last=False):
         bias = bias_of(start, count)
 
-        def head(h):
-            cols = pl.ds(pl.multiple_of(h * HEAD_DIM, HEAD_DIM), HEAD_DIM)
-            s = lax.dot_general(
-                q[:, cols], kbuf[pl.ds(start, count), cols], (((1,), (1,)), ((), ())),
-                preferred_element_type=jnp.float32,
-            ) * scale
-            if bias is not None:
-                s = s + bias
-            peak = jnp.max(s, axis=-1, keepdims=True)
+        def block(first_head):
+            cols = [
+                pl.ds(pl.multiple_of((first_head + u) * HEAD_DIM, HEAD_DIM), HEAD_DIM)
+                for u in range(UNROLL)
+            ]
+            scores = [
+                lax.dot_general(
+                    q[:, c], kbuf[pl.ds(start, count), c], (((1,), (1,)), ((), ())),
+                    preferred_element_type=jnp.float32,
+                )
+                for c in cols
+            ]
+            scores = [s * scale if bias is None else s * scale + bias for s in scores]
+            peaks = [jnp.max(s, axis=-1, keepdims=True) for s in scores]
             if first:
-                old, new = None, jnp.broadcast_to(peak, (64, HEAD_DIM))
+                tops = [jnp.broadcast_to(peak, (64, HEAD_DIM)) for peak in peaks]
             else:
-                old = top[:, cols]
-                new = jnp.maximum(old, peak)
-            p = jnp.exp2(s - new[:, :count])
-            add = jnp.dot(
-                p.astype(jnp.bfloat16), vbuf[pl.ds(start, count), cols],
-                preferred_element_type=jnp.float32,
-            )
+                olds = [top[:, c] for c in cols]
+                tops = [jnp.maximum(old, peak) for old, peak in zip(olds, peaks)]
+                keeps = [jnp.exp2(old - new) for old, new in zip(olds, tops)]
+            weights = [jnp.exp2(s - new[:, :count]) for s, new in zip(scores, tops)]
+            values = [
+                jnp.dot(
+                    p.astype(jnp.bfloat16), vbuf[pl.ds(start, count), c],
+                    preferred_element_type=jnp.float32,
+                )
+                for p, c in zip(weights, cols)
+            ]
             if count < HEAD_DIM:
-                p = jnp.concatenate([p, jnp.zeros((64, HEAD_DIM - count), jnp.float32)], axis=1)
-            if first:
-                total, value = p, add
+                rest = jnp.zeros((64, HEAD_DIM - count), jnp.float32)
+                weights = [jnp.concatenate([p, rest], axis=1) for p in weights]
+            if not first:
+                weights = [part[:, c] * keep + p for c, keep, p in zip(cols, keeps, weights)]
+                values = [acc[:, c] * keep + v for c, keep, v in zip(cols, keeps, values)]
+            if last:
+                totals = [jnp.sum(p, axis=-1, keepdims=True) for p in weights]
+                for c, total, value in zip(cols, totals, values):
+                    out_ref[:, c] = (value / total).astype(jnp.bfloat16)
             else:
-                keep = jnp.exp2(old - new)
-                total = part[:, cols] * keep + p
-                value = acc[:, cols] * keep + add
-            if last:
-                total = jnp.sum(total, axis=-1, keepdims=True)
-                out_ref[:, cols] = (value / total).astype(jnp.bfloat16)
-            else:
-                top[:, cols] = new
-                part[:, cols] = total
-                acc[:, cols] = value
+                for c, new, p, value in zip(cols, tops, weights, values):
+                    top[:, c] = new
+                    part[:, c] = p
+                    acc[:, c] = value
 
         @pl.loop(0, heads // UNROLL)
         def _(step):
-            for u in range(UNROLL):
-                head(step * UNROLL + u)
+            block(step * UNROLL)
 
     for load in loads[2:]:
         load.wait()
+    landed("other", OTHER)
+    attend(OWN, 128, first=True)
+    ring("own", 1)
+    pl.when(z == 0)(open_z)
+    sent.extend(
+        remote(("zd", kv, n), piece(fresh[kv], n), tile(kv, ZD, n), zdirect) for kv, n in every
+    )
+    pass_x(0, 0)
+    ring("own", 2)
     for kv in (0, 1):
-        arrived(("other", kv), rows(kv, OTHER, 64))
-    attend(OWN, 128, first=True)
-    for kv in (0, 1):
-        arrived(("par0", kv), rows(kv, POOLED[("par", 0, 0)], 16))
         block = rows(kv, POOLED[("par", 0, 0)], 16)
+        arrived(("par0", kv), block)
         for way in (1, -1):
             send(("par", 1, way, kv), block, rows(kv, POOLED[("par", 1, way)], 16), ynext[way])
-    ring("own", 1)
-    for kv in (0, 1):
-        tile = rows(kv, X, 64)
-        arrived(("x", kv), tile)
-        send(("zf", kv), tile, rows(kv, ZF, 64), zforward)
-        send(("xf", kv), tile, rows(kv, XF, 64), other)
-    for kv in (0, 1):
-        arrived(("zd", kv), rows(kv, ZD, 64))
+    pass_x(0, 1)
+    landed("zd", ZD)
     attend(ZD, 128)
+    ring("own", 3)
+    pass_x(1, 0)
     ring("par", 1)
-    ring("own", 2)
-    for kv in (0, 1):
-        arrived(("xf", kv), rows(kv, XF, 64))
+    pass_z(0, 0)
+    pass_far(0)
+    pass_far(1)
+    pass_x(1, 1)
+    pass_z(0, 1)
+    landed("xf", XF)
     attend(X, 128)
     ring("par", 2)
-    for kv in (0, 1):
-        tile = rows(kv, ZF, 64)
-        arrived(("zf", kv), tile)
-        send(("zff", kv), tile, rows(kv, ZFF, 64), other)
-    for kv in (0, 1):
-        arrived(("zff", kv), rows(kv, ZFF, 64))
+    pass_z(1, 0)
+    attend(POOLED[("own", 2, 1)], 128)
+    pass_z(1, 1)
+    landed("zff", ZFF)
     attend(ZF, 128)
-    ring("own", 3)
-    attend(POOLED[("par", 1, 1)], 128)
     ring("par", 3)
     for kv in (0, 1):
-        for col in ("own", "par"):
-            arrived((col, 4, 1, kv), rows(kv, POOLED[(col, 4, 1)], 16))
-    attend(POOLED[("par", 3, 1)], 64, last=True)
+        arrived(("par", 4, 1, kv), rows(kv, POOLED[("par", 4, 1)], 16))
+    attend(POOLED[("par", 2, -1)], 64, last=True)
     for copy in sent:
         copy.wait_send()
 
@@ -287,6 +349,7 @@
             pltpu.SemaphoreType.DMA((copies,)),
             pltpu.SemaphoreType.DMA((copies,)),
             pltpu.SemaphoreType.DMA((5,)),
+            pltpu.SemaphoreType.REGULAR,
         ],
         name="tile_attention",
         compiler_params=pltpu.CompilerParams(

time: 68.6 us -> 45.6 us (0.66)
  Pallas kernels: 66.7 us -> 43.6 us
    pallas_call x1, Pallas kernels: 66.7 us -> 43.6 us  [body(): pl.pallas_call(kernel, out_shape=jax.ShapeDtypeStruct(wide, jnp.bfloat16)...]
where the time goes in v2:
time: 45.6 us; the launch traced here: 45.4 us
  Pallas kernels  43.6 us (96%)
  local copies, waits for them, and re-layouts  1.72 us (4%)
    pallas_call x1, Pallas kernels, body(): pl.pallas_call(kernel, out_shape=jax.ShapeDtypeStruct(wide, jnp.bfloat16)...  43.6 us
    unnamed x1, local copies, waits for them, and re-layouts  1.72 us

profile of v2, /device:TPU:1, one launch (start us, length us, event | category | flops | bytes accessed | tf_op | source)
XLA Modules:
  0.0 45.4 jit_solution(12305101602183630871)
XLA Ops:
  0.0 43.6 %tile_attention.1 = bf16[64,2560]{1,0:T(8,128)(2,1)} custom-call(bf16[64,2560]{1,0:T(8,128)(2,1)} %q_hbm.1, bf16[64,2560]{1,0:T(8,128)(2,1)} %k_hbm.1, bf16[64,2560]{1,0:T(8,128)(2,1)} %v_hbm.1, bf16[64,2560]{1,0:T(8,128)(2,1)} %sk_hbm.1, bf16[64,2560]{1,0:T(8,128)(2,1)} %sv_hbm.1, s32[1,64]{1,0:T(1,128)} %bitcast.1, s32[16]{0:T(128)} %age_ref.1), custom_call_target="tpu_custom_call" | custom-call | tf_op jit(solution)/shard_map/tile_attention/pallas_call | solution.py:334
  43.7 1.7 %copy.9 = bf16[64,2560]{1,0:T(8,128)(2,1)} copy(bf16[64,2560]{1,0:T(8,128)(2,1)} %tile_attention.1) | data formatting | bytes 655360

commit v3 on v2

--- a/solution.py
+++ b/solution.py
@@ -104,7 +104,7 @@
             )
         )
     ]
-    for load in loads:
+    for load in loads[:2]:
         load.start()
 
     def rows(kv, slot, count):
@@ -136,23 +136,32 @@
         quarter, picks, (((1,), (1,)), ((), ())), preferred_element_type=jnp.float32
     ).astype(jnp.bfloat16)
     mine = POOLED[("own", 0, 0)]
-    for kv, stale in enumerate((sk, sv)):
+
+    def pool(kv):
         loads[kv].wait()
         bufs[kv][pl.ds(mine, 16), :] = jnp.dot(
-            average, stale[...], preferred_element_type=jnp.float32
+            average, (sk, sv)[kv][...], preferred_element_type=jnp.float32
         ).astype(jnp.bfloat16)
 
-    pl.semaphore_wait(barrier, len(plane) + len(across) * odd)
-
-    @pl.when(odd == 1)
-    def _():
-        signal(zsem, across)
-
-    for kv in (0, 1):
+    def send_pooled(kv):
         block = rows(kv, mine, 16)
         for way in (1, -1):
             send(("own", 1, way, kv), block, rows(kv, POOLED[("own", 1, way)], 16), ynext[way])
         send(("par0", kv), block, rows(kv, POOLED[("par", 0, 0)], 16), partner)
+
+    pool(0)
+    pl.semaphore_wait(barrier, len(plane) + len(across) * odd)
+
+    @pl.when(odd == 1)
+    def _():
+        signal(zsem, across)
+
+    send_pooled(0)
+    pool(1)
+    send_pooled(1)
+    for load in loads[2:]:
+        load.start()
+
     span = q.shape[1] // PARTS
 
     def piece(ref, part):
@@ -333,7 +342,7 @@
     wide = (rows, width)
     return pl.pallas_call(
         kernel,
-        out_shape=jax.ShapeDtypeStruct(wide, jnp.bfloat16),
+        out_shape=pltpu.VMEM(wide, jnp.bfloat16),
         in_specs=[pl.BlockSpec(memory_space=pl.ANY)] * 5
         + [pl.BlockSpec(memory_space=pltpu.VMEM), pl.BlockSpec(memory_space=pltpu.SMEM)],
         out_specs=pl.BlockSpec(memory_space=pltpu.VMEM),

time: 45.6 us -> 43.8 us (0.961)
  local copies, waits for them, and re-layouts: 1.72 us -> 0.73 us
  Pallas kernels: 43.6 us -> 42.9 us
    unnamed x1, local copies, waits for them, and re-layouts: 1.72 us -> 0.73 us
    pallas_call x1, Pallas kernels: 43.6 us -> 42.9 us  [body(): pl.pallas_call(kernel, out_shape=pltpu.VMEM(wide, jnp.bfloat16), in_specs...]
where the time goes in v3:
time: 43.8 us; the launch traced here: 43.7 us
  Pallas kernels  42.9 us (98%)
  local copies, waits for them, and re-layouts  0.73 us (2%)
    pallas_call x1, Pallas kernels, body(): pl.pallas_call(kernel, out_shape=pltpu.VMEM(wide, jnp.bfloat16), in_specs...  42.9 us

profile of v3, /device:TPU:1, one launch (start us, length us, event | category | flops | bytes accessed | tf_op | source)
XLA Modules:
  0.0 43.7 jit_solution(13836489706177902889)
XLA Ops:
  0.0 42.9 %tile_attention.1 = bf16[64,2560]{1,0:T(8,128)(2,1)S(1)} custom-call(bf16[64,2560]{1,0:T(8,128)(2,1)} %q_hbm.1, bf16[64,2560]{1,0:T(8,128)(2,1)} %k_hbm.1, bf16[64,2560]{1,0:T(8,128)(2,1)} %v_hbm.1, bf16[64,2560]{1,0:T(8,128)(2,1)} %sk_hbm.1, bf16[64,2560]{1,0:T(8,128)(2,1)} %sv_hbm.1, s32[1,64]{1,0:T(1,128)} %bitcast.1, s32[16]{0:T(128)} %age_ref.1), custom_call_target="tpu_custom_call" | custom-call | tf_op jit(solution)/shard_map/tile_attention/pallas_call | solution.py:343
  43.0 0.7 %copy.9 = bf16[64,2560]{1,0:T(8,128)(2,1)} copy(bf16[64,2560]{1,0:T(8,128)(2,1)S(1)} %tile_attention.1) | data formatting | bytes 655360

commit v4 on v3

--- a/solution.py
+++ b/solution.py
@@ -75,21 +75,6 @@
     ynext = {1: at(xh, (y + 1) % 8, z, xl, c), -1: at(xh, (y + 7) % 8, z, xl, c)}
     partner = at(1 - xh, y, z, xl, c)
 
-    barrier = pltpu.get_barrier_semaphore()
-    plane = (other, xpeer, ynext[1], ynext[-1], partner)
-    across = (zup, zdown, zdirect)
-    odd = z % 2
-
-    def signal(semaphore, devices):
-        for device in devices:
-            pl.semaphore_signal(semaphore, inc=1, device_id=device, device_id_type=MESH)
-
-    signal(barrier, plane)
-
-    @pl.when(odd == 0)
-    def _():
-        signal(barrier, across)
-
     bufs = (kbuf, vbuf)
     fresh = (k_hbm, v_hbm)
     loads = [
@@ -106,6 +91,21 @@
     ]
     for load in loads[:2]:
         load.start()
+
+    barrier = pltpu.get_barrier_semaphore()
+    plane = (other, xpeer, ynext[1], ynext[-1], partner)
+    across = (zup, zdown, zdirect)
+    odd = z % 2
+
+    def signal(semaphore, devices):
+        for device in devices:
+            pl.semaphore_signal(semaphore, inc=1, device_id=device, device_id_type=MESH)
+
+    signal(barrier, plane)
+
+    @pl.when(odd == 0)
+    def _():
+        signal(barrier, across)
 
     def rows(kv, slot, count):
         return bufs[kv].at[pl.ds(slot, count)]
@@ -326,12 +326,12 @@
     pass_z(1, 0)
     attend(POOLED[("own", 2, 1)], 128)
     pass_z(1, 1)
-    landed("zff", ZFF)
-    attend(ZF, 128)
     ring("par", 3)
     for kv in (0, 1):
         arrived(("par", 4, 1, kv), rows(kv, POOLED[("par", 4, 1)], 16))
-    attend(POOLED[("par", 2, -1)], 64, last=True)
+    attend(POOLED[("par", 2, -1)], 64)
+    landed("zff", ZFF)
+    attend(ZF, 128, last=True)
     for copy in sent:
         copy.wait_send()
 

time: 43.8 us -> 43.2 us (0.986)
  Pallas kernels: 42.9 us -> 42.3 us
    pallas_call x1, Pallas kernels: 42.9 us -> 42.3 us  [body(): pl.pallas_call(kernel, out_shape=pltpu.VMEM(wide, jnp.bfloat16), in_specs...]
where the time goes in v4:
time: 43.2 us; the launch traced here: 43.1 us
  Pallas kernels  42.3 us (98%)
  local copies, waits for them, and re-layouts  0.73 us (2%)
    pallas_call x1, Pallas kernels, body(): pl.pallas_call(kernel, out_shape=pltpu.VMEM(wide, jnp.bfloat16), in_specs...  42.3 us

profile of v4, /device:TPU:1, one launch (start us, length us, event | category | flops | bytes accessed | tf_op | source)
XLA Modules:
  0.0 43.1 jit_solution(6267686942492028063)
XLA Ops:
  0.0 42.3 %tile_attention.1 = bf16[64,2560]{1,0:T(8,128)(2,1)S(1)} custom-call(bf16[64,2560]{1,0:T(8,128)(2,1)} %q_hbm.1, bf16[64,2560]{1,0:T(8,128)(2,1)} %k_hbm.1, bf16[64,2560]{1,0:T(8,128)(2,1)} %v_hbm.1, bf16[64,2560]{1,0:T(8,128)(2,1)} %sk_hbm.1, bf16[64,2560]{1,0:T(8,128)(2,1)} %sv_hbm.1, s32[1,64]{1,0:T(1,128)} %bitcast.1, s32[16]{0:T(128)} %age_ref.1), custom_call_target="tpu_custom_call" | custom-call | tf_op jit(solution)/shard_map/tile_attention/pallas_call | solution.py:343
  42.4 0.7 %copy.9 = bf16[64,2560]{1,0:T(8,128)(2,1)} copy(bf16[64,2560]{1,0:T(8,128)(2,1)S(1)} %tile_attention.1) | data formatting | bytes 655360

commit v5 on v4

--- a/solution.py
+++ b/solution.py
@@ -293,10 +293,6 @@
         def _(step):
             block(step * UNROLL)
 
-    for load in loads[2:]:
-        load.wait()
-    landed("other", OTHER)
-    attend(OWN, 128, first=True)
     ring("own", 1)
     pl.when(z == 0)(open_z)
     sent.extend(
@@ -309,6 +305,10 @@
         arrived(("par0", kv), block)
         for way in (1, -1):
             send(("par", 1, way, kv), block, rows(kv, POOLED[("par", 1, way)], 16), ynext[way])
+    for load in loads[2:]:
+        load.wait()
+    landed("other", OTHER)
+    attend(OWN, 128, first=True)
     pass_x(0, 1)
     landed("zd", ZD)
     attend(ZD, 128)

time: 43.2 us -> 43.4 us (level)
  no operation moved by 1% of the time
where the time goes in v5:
time: 43.4 us; the launch traced here: 43.3 us
  Pallas kernels  42.5 us (98%)
  local copies, waits for them, and re-layouts  0.73 us (2%)
    pallas_call x1, Pallas kernels, body(): pl.pallas_call(kernel, out_shape=pltpu.VMEM(wide, jnp.bfloat16), in_specs...  42.5 us

profile of v5, /device:TPU:1, one launch (start us, length us, event | category | flops | bytes accessed | tf_op | source)
XLA Modules:
  0.0 43.3 jit_solution(9070652310468851666)
XLA Ops:
  0.0 42.5 %tile_attention.1 = bf16[64,2560]{1,0:T(8,128)(2,1)S(1)} custom-call(bf16[64,2560]{1,0:T(8,128)(2,1)} %q_hbm.1, bf16[64,2560]{1,0:T(8,128)(2,1)} %k_hbm.1, bf16[64,2560]{1,0:T(8,128)(2,1)} %v_hbm.1, bf16[64,2560]{1,0:T(8,128)(2,1)} %sk_hbm.1, bf16[64,2560]{1,0:T(8,128)(2,1)} %sv_hbm.1, s32[1,64]{1,0:T(1,128)} %bitcast.1, s32[16]{0:T(128)} %age_ref.1), custom_call_target="tpu_custom_call" | custom-call | tf_op jit(solution)/shard_map/tile_attention/pallas_call | solution.py:343
  42.5 0.7 %copy.9 = bf16[64,2560]{1,0:T(8,128)(2,1)} copy(bf16[64,2560]{1,0:T(8,128)(2,1)S(1)} %tile_attention.1) | data formatting | bytes 655360
